TPU v7x, 32 devices: a whole 2x2x4 slice. The times are simulated.
32 devices in a mesh: seq: 2 (over x), ctx: 4 (over y, core), head: 4 (over z).
Axes of the slice: x: 2, y: 2, z: 4, core: 2. Of those that a mesh axis runs over, the one named last changes fastest.
Arguments:
- queries: bfloat16 [1536, 6144], P(('seq', 'ctx'), 'head'), parts along dimension 0, may hold values from -210 to 210
- kv_latent: bfloat16 [1536, 576], P(('seq', 'ctx')), parts along dimension 0, may hold values from -6 to 6
- kv_gain: float32 [512], replicated, may hold values from 0.25 to 1.75
- w_ukv: bfloat16 [512, 8192], P(None, 'head'), may hold values from -0.25 to 0.25
- w_out: bfloat16 [4096, 7168], P('head', 'ctx'), may hold values from -0.125 to 0.125
- row_position: int32 [1536], P('seq'), parts along dimension 0, may hold values from 0 to 767, as said below
Outputs:
- mixed: bfloat16 [1536, 7168], P(('seq', 'ctx'), 'head'), parts along dimension 0
There are 2 independent parts, one for each index of `seq`. A program takes and returns all parts, laid end to end along the dimension named above; an argument that names none is the same for every part. Nothing has to cross between parts.
Inputs may be any that keep to these rules, and one draw needn't show every extreme that they name: `row_position`: the 768 values are a permutation of the positions. The rows of one index of ctx are two runs of 96 consecutive positions, the blocks b and 7 - b of the sequence cut into blocks of 96 positions, in either order.
All inputs are finite; a program needn't handle non-finite values.
Results may differ from a plain program's by a relative error of at most 0.012.
Values may be sent and summed in bfloat16 or wider, within the bound.
A program may use at most 128 MiB of HBM per device.

v0:
```python
import jax
import jax.numpy as jnp
from jax import lax
from jax.sharding import PartitionSpec as P

KVR = 512
NOPE = 128
ROPE = 64
VDIM = 128


def normalize(kv_latent, kv_gain):
    rows = kv_latent.astype(jnp.float32)
    front = rows[:, :KVR]
    factor = lax.rsqrt(jnp.mean(front * front, axis=1, keepdims=True) + 1e-06)
    return jnp.concatenate([front * factor * kv_gain, rows[:, KVR:]], axis=1).astype(jnp.bfloat16)


def attend_piece(state, piece, key_pos, q_heads, own_pos, w_ukv):
    heads = q_heads.shape[1]
    length = piece.shape[0]
    factor_score = (NOPE + ROPE) ** (-0.5)
    for begin in range(0, length, 1024):
        size = min(1024, length - begin)
        rows = piece[begin : begin + size]
        positions = key_pos[begin : begin + size]
        peak, mass, acc = state
        expanded = jnp.dot(rows[:, :KVR], w_ukv, preferred_element_type=jnp.float32).astype(
            jnp.bfloat16
        )
        expanded = expanded.reshape(size, heads, NOPE + VDIM)
        scores = jnp.einsum(
            "qhd,khd->qhk",
            q_heads[:, :, :NOPE],
            expanded[:, :, :NOPE],
            preferred_element_type=jnp.float32,
        )
        scores = scores + jnp.einsum(
            "qhd,kd->qhk", q_heads[:, :, NOPE:], rows[:, KVR:], preferred_element_type=jnp.float32
        )
        scores = scores * factor_score
        allowed = (positions[None, :] <= own_pos[:, None])[:, None, :]
        scores = jnp.where(allowed, scores, -1e30)
        new_peak = jnp.maximum(peak, jnp.max(scores, axis=2))
        shrink = jnp.exp(peak - new_peak)
        probs = jnp.where(allowed, jnp.exp(scores - new_peak[:, :, None]), 0.0)
        mass = mass * shrink + jnp.sum(probs, axis=2)
        added = jnp.einsum(
            "qhk,khd->qhd",
            probs.astype(jnp.bfloat16),
            expanded[:, :, NOPE:],
            preferred_element_type=jnp.float32,
        )
        acc = acc * shrink[:, :, None] + added
        state = (new_peak, mass, acc)
    return state


def shards(queries, kv_latent, kv_gain, w_ukv, w_out, row_position):
    tok_rows = queries.shape[0]
    heads = w_ukv.shape[1] // (NOPE + VDIM)
    ctx_index = lax.axis_index("ctx")
    own_pos = lax.dynamic_slice_in_dim(row_position, ctx_index * tok_rows, tok_rows)
    latent = normalize(kv_latent, kv_gain)
    q_heads = queries.reshape(tok_rows, heads, NOPE + ROPE)
    start_state = (
        jnp.full((tok_rows, heads), -1e30, jnp.float32),
        jnp.zeros((tok_rows, heads), jnp.float32),
        jnp.zeros((tok_rows, heads, VDIM), jnp.float32),
    )
    every = lax.all_gather(latent, "ctx", axis=0, tiled=True)
    state = attend_piece(start_state, every, row_position, q_heads, own_pos, w_ukv)
    peak, mass, acc = state
    attended = (acc / mass[:, :, None]).astype(jnp.bfloat16).reshape(tok_rows, heads * VDIM)
    terms = jnp.dot(
        attended,
        lax.all_gather(w_out, "ctx", axis=1, tiled=True),
        preferred_element_type=jnp.float32,
    )
    return lax.psum_scatter(terms.astype(jnp.bfloat16), "head", scatter_dimension=1, tiled=True)


def solution(mesh):
    placed = (
        P(("seq", "ctx"), "head"),
        P(("seq", "ctx"), None),
        P(),
        P(None, "head"),
        P("head", "ctx"),
        P("seq"),
    )
    return jax.shard_map(
        shards, mesh=mesh, in_specs=placed, out_specs=P(("seq", "ctx"), "head"), check_vma=False
    )
```

profile of v0, /device:TPU:0, one launch (start us, length us, event | category | flops | bytes accessed | tf_op | source)
XLA Modules:
  0.0 176.5 jit_solution(8931286480442797836)
XLA Ops:
  6.5 0.0 copy-start
  6.5 0.0 copy-start.3
  6.5 0.0 slice-start.2
  6.5 0.0 copy-start.5
  6.5 0.0 all-gather.2.cloned.1.call-start
  6.6 0.7 all-gather.2.cloned.1.call-update
  7.3 0.0 reduce-scatter.2.cloned.1.call-start
  7.3 1.7 reshape.55
  9.1 0.0 copy-start.1
  9.1 0.0 copy-done.3
  9.1 0.1 fusion.38
  9.2 0.0 copy-done.5
  9.2 0.1 fusion.40
  9.4 0.0 slice-done.2
  9.4 11.1 %all_gather.6 = bf16[768,576]{1,0:T(8,128)(2,1)S(1)} all-gather(bf16[192,576]{1,0:T(8,128)(2,1)S(1)} %pad_maximum_fusion), channel_id=1, replica_groups=mesh['seq'=2,'ctx'=4,'head'=4] {'ctx'}, dimensions={0}, use_global_device_ids=true | all-gather | bytes 1105920 | tf_op jit(solution)/shard_map/all_gather | solution.py:71
  20.5 0.0 copy-start.2
  20.5 1.0 copy-done.2
  21.5 0.0 copy-done
  21.5 1.8 %convolution_convert_fusion.1 = bf16[768,2048]{1,0:T(8,128)(2,1)S(1)} fusion(bf16[512,2048]{1,0:T(8,128)(2,1)S(1)} %copy-done, bf16[768,576]{1,0:T(8,128)(2,1)S(1)} %all_gather.6), kind=kOutput, calls=%fused_computation.7 | convolution fusion | flops 1612185600 | bytes 6029312 | tf_op jit(solution)/shard_map/dot_general | solution.py:28
  23.4 0.0 copy-done.1
  23.4 0.0 copy-start.4
  23.4 3.2 %copy.31 = bf16[96,8,8,256]{3,2,1,0:T(8,128)(2,1)} copy(bf16[96,8,8,256]{3,1,2,0:T(8,128)(2,1)S(1)} %bitcast.34) | data formatting | bytes 6291456
  26.6 0.0 slice-start
  26.6 0.0 copy-done.4
  26.6 0.1 dynamic_slice.3
  26.7 0.2 broadcast_compare_fusion
  26.8 2.7 %fusion.47 = (bf16[768,8,128]{2,1,0:T(8,128)(2,1)S(1)}, bf16[768,8,128]{2,1,0:T(8,128)(2,1)S(1)}) fusion(bf16[768,8,256]{2,1,0:T(8,128)(2,1)} %bitcast.33), kind=kLoop, calls=%fused_computation.38 | loop fusion | bytes 6291456 | tf_op jit(solution)/shard_map/slice | solution.py:35
  29.5 0.0 slice-start.1
  29.6 0.0 slice-done
  29.6 0.8 fusion.10
  30.4 0.2 slice-done.1
  30.5 2.3 %fusion.48 = (f32[192,8]{0,1:T(8,128)S(1)}, f32[192,8,768]{2,0,1:T(8,128)S(1)}) fusion(bf16[192,8,64]{2,1,0:T(8,128)(2,1)S(1)} %slice-done.1, bf16[768,576]{1,0:T(8,128)(2,1)} %copy-done.2, f32[8,768,192]{1,2,0:T(8,128)S(1)} %fusion.10, pred[192,768]{1,0:T(8,128)(4,1)S(1)} %broadcast_compare_fusion), kind=kOutput, calls=%fused_computation.39 | convolution fusion | flops 155712000 | bytes 9984000 | tf_op jit(solution)/shard_map/qhd,kd->qhk/dot_general | solution.py:38
  32.9 1.6 fusion.2
  34.5 1.7 fusion.32
  36.2 69.5 %all-gather.2.cloned.1.call-done = bf16[1024,7168]{1,0:T(8,128)(2,1)} async-done(((bf16[1024,1792]{1,0:T(8,128)(2,1)}), bf16[1024,7168]{1,0:T(8,128)(2,1)}) %all-gather.2.cloned.1.call-update) | async-done | bytes 14680080 | tf_op jit(solution)/shard_map/all_gather | solution.py:77
  105.7 9.7 %convolution_convert_fusion = bf16[192,7168]{1,0:T(8,128)(2,1)} fusion(bf16[1024,7168]{1,0:T(8,128)(2,1)} %all-gather.2.cloned.1.call-done, bf16[8,24,8,128]{3,2,1,0:T(8,128)(2,1)S(1)} %fusion.32), kind=kOutput, calls=%fused_computation | convolution fusion | flops 2819948544 | bytes 17825792 | tf_op jit(solution)/shard_map/dot_general | solution.py:75
  115.4 0.0 reduce-scatter.2.cloned.1.call-update
  115.4 54.3 %reduce-scatter.2.cloned.1.call-done = bf16[192,1792]{1,0:T(8,128)(2,1)} async-done(((bf16[192,7168]{1,0:T(8,128)(2,1)}), bf16[192,1792]{1,0:T(8,128)(2,1)}) %reduce-scatter.2.cloned.1.call-update) | async-done | bytes 688144 | tf_op jit(solution)/shard_map/reduce_scatter | solution.py:80
  (4 shorter events, 0.0 us)
Async XLA Ops:
  6.5 15.0 %copy-start = (bf16[512,2048]{1,0:T(8,128)(2,1)S(1)}, bf16[512,2048]{1,0:T(8,128)(2,1)}, u32[]{:S(2)}) copy-start(bf16[512,2048]{1,0:T(8,128)(2,1)} %param.9) | copy-start | bytes 6291460
  6.5 2.5 %copy-start.3 = (bf16[192,576]{1,0:T(8,128)(2,1)S(1)}, bf16[192,576]{1,0:T(8,128)(2,1)}, u32[]{:S(2)}) copy-start(bf16[192,576]{1,0:T(8,128)(2,1)} %param.7) | copy-start | bytes 663556
  6.5 2.8 %slice-start.2 = ((bf16[192,576]{1,0:T(8,128)(2,1)}), bf16[192,64]{1,0:T(8,128)(2,1)S(1)}, s32[]{:S(2)}) async-start(bf16[192,576]{1,0:T(8,128)(2,1)} %param.7), calls=%async_computation.5 | async-start | bytes 98304 | tf_op jit(solution)/shard_map/slice | solution.py:16
  6.5 2.7 %copy-start.5 = (f32[512]{0:T(512)S(1)}, f32[512]{0:T(512)}, u32[]{:S(2)}) copy-start(f32[512]{0:T(512)} %param.8) | copy-start | bytes 6148
  6.5 99.1 %all-gather.2.cloned.1.call-start = ((), (), s32[]{:S(2)}) async-start(), calls=%async_computation.1 | async-start | bytes 18350080 | tf_op jit(solution)/shard_map/all_gather | solution.py:77
  7.3 162.4 %reduce-scatter.2.cloned.1.call-start = ((), (), s32[]{:S(2)}) async-start(), calls=%async_computation.2 | async-start | bytes 3440640 | tf_op jit(solution)/shard_map/reduce_scatter | solution.py:80
  9.1 14.3 %copy-start.1 = (bf16[192,8,192]{2,1,0:T(8,128)(2,1)}, bf16[192,8,192]{2,1,0:T(8,128)(2,1)S(1)}, u32[]{:S(2)}) copy-start(bf16[192,8,192]{2,1,0:T(8,128)(2,1)S(1)} %reshape.55) | copy-start | bytes 1769476
  20.5 1.0 copy-start.2
  23.4 3.2 %copy-start.4 = (s32[768]{0:T(1024)S(1)}, s32[768]{0:T(1024)}, u32[]{:S(2)}) copy-start(s32[768]{0:T(1024)} %param.11) | copy-start | bytes 9220
  26.6 3.0 %slice-start = ((bf16[192,8,192]{2,1,0:T(8,128)(2,1)}), bf16[192,8,128]{2,1,0:T(8,128)(2,1)S(1)}, s32[]{:S(2)}) async-start(bf16[192,8,192]{2,1,0:T(8,128)(2,1)} %copy-done.1), calls=%async_computation.3 | async-start | bytes 786432 | tf_op jit(solution)/shard_map/slice | solution.py:34
  29.5 1.0 slice-start.1
Sparse Core Ops, SparseCore 0:
  8.9 96.7 all-gather.1
  115.5 54.1 reduce-scatter.1
where the time goes:
time: 177 us
  waiting for transfers between devices  124 us (70%)
  matrix products  16.3 us (9%)
  between operations  13.6 us (8%)
  blocking collectives  11.1 us (6%)
  local copies, waits for them, and re-layouts  8.93 us (5%)
  other arithmetic  2.04 us (1%)
    all_gather x1, waiting for transfers between devices, shards(): lax.all_gather(w_out, 'ctx', axis=1, tiled=True)  69.5 us
    reduce_scatter x1, waiting for transfers between devices, shards(): lax.psum_scatter(terms.astype(jnp.bfloat16), 'head', scatter_dimension=1,...  54.3 us
    all_gather x1, blocking collectives, shards(): every = lax.all_gather(latent, 'ctx', axis=0, tiled=True)  11.1 us
    dot_general x1, matrix products, shards(): jnp.dot(attended, lax.all_gather(w_out, 'ctx', axis=1, tiled=True), prefe...  9.69 us
    unnamed x13, local copies, waits for them, and re-layouts  4.2 us
  transfers between devices with their start and end apart: 2, of which 2 were waited for; matrix products, arithmetic and copies ran while one was open for 9% of the time, Pallas kernels for 0%

commit v1 on v0

v1 whole, which is shorter than its diff:
```python
import functools
import math

import jax
import jax.numpy as jnp
from jax import lax
from jax.experimental import pallas as pl
from jax.experimental.pallas import tpu as pltpu
from jax.sharding import PartitionSpec as P

KVR = 512
NOPE = 128
ROPE = 64
VDIM = 128
LAT = 640
CW = 256
F32 = jnp.float32
BF16 = jnp.bfloat16


def normalize(kv_latent, kv_gain):
    rows = kv_latent.astype(F32)
    front = rows[:, :KVR]
    factor = lax.rsqrt(jnp.mean(front * front, axis=1, keepdims=True) + 1e-06)
    return jnp.concatenate([front * factor * kv_gain, rows[:, KVR:]], axis=1).astype(BF16)


def layer_kernel(
    q_ref, kvl_ref, gain_ref, ukv_ref, own_pos_ref, key_pos_ref, wout_ref, out_ref,
    lat, keys, values, bias, att, w, pown, outbox, inbox,
    local_sem, lat_s, lat_r, core_s, core_r, y_s, y_r, x_s, x_r, cy_s, cy_r, cx_s, cx_r, ob_s, ib_r,
):
    x = lax.axis_index("seq")
    c = lax.axis_index("ctx")
    z = lax.axis_index("head")
    y = c // 2
    k = c % 2
    c_core = y * 2 + (1 - k)
    c_y = (1 - y) * 2 + k
    c_yc = (1 - y) * 2 + (1 - k)
    side = z // 2
    is_edge = (z % 2) == side
    partner = z + 1 - 2 * (z % 2)
    mid_far = 2 - side
    end_far = 3 * (1 - side)

    heads = values.shape[0]
    tok = q_ref.shape[0]
    depth, width = wout_ref.shape
    half = depth // 2
    chunks = width // CW
    qd = NOPE + ROPE

    core_id = (x, c_core, z)
    y_id = (x, c_y, z)
    x_id = (1 - x, c, z)

    barrier = pltpu.get_barrier_semaphore()
    for peer in (core_id, y_id, x_id, (x, c, partner), (x, c, mid_far), (x, c, end_far)):
        pl.semaphore_signal(barrier, inc=1, device_id=peer, device_id_type=pl.DeviceIdType.MESH)

    own_w = pltpu.make_async_copy(wout_ref, w.at[c], local_sem)
    own_w.start()

    raw = kvl_ref[...].astype(F32)
    front = raw[:, :KVR]
    factor = lax.rsqrt(jnp.mean(front * front, axis=1, keepdims=True) + 1e-06)
    lat[c, :, :KVR] = (front * factor * gain_ref[...]).astype(BF16)
    lat[c, :, KVR:] = jnp.concatenate(
        [kvl_ref[:, KVR:], jnp.zeros((tok, LAT - KVR - ROPE), BF16)], axis=1
    )
    pl.semaphore_wait(barrier, 6)

    def remote(src, dst, send, recv, dev):
        return pltpu.make_async_remote_copy(
            src_ref=src, dst_ref=dst, send_sem=send, recv_sem=recv,
            device_id=dev, device_id_type=pl.DeviceIdType.MESH,
        )

    def lat_copy(block, slot, dev):
        return remote(lat.at[block], lat.at[block], lat_s.at[slot], lat_r.at[slot], dev)

    lat_copy(c, 1, y_id).start()
    lat_copy(c, 0, core_id).start()
    own_to_core = remote(wout_ref, w.at[c], core_s, core_r, core_id)
    own_to_core.start()

    def part(block, which, n):
        rows = pl.ds(pl.multiple_of(which * half, half), half)
        return w.at[block, rows, pl.ds(pl.multiple_of(n * CW, CW), CW)]

    def y_copy(n):
        rows = pl.ds(pl.multiple_of(x * half, half), half)
        src = wout_ref.at[rows, pl.ds(pl.multiple_of(n * CW, CW), CW)]
        return remote(src, part(c, x, n), y_s.at[n], y_r.at[n], y_id)

    def y_in(n):
        return remote(part(c_y, x, n), part(c_y, x, n), y_s.at[n], y_r.at[n], y_id)

    def x_copy(n):
        return remote(part(c_y, x, n), part(c_y, x, n), x_s.at[n], x_r.at[n], x_id)

    def x_in(n):
        return remote(part(c_y, 1 - x, n), part(c_y, 1 - x, n), x_s.at[n], x_r.at[n], x_id)

    def cy_copy(n):
        return remote(part(c_y, x, n), part(c_y, x, n), cy_s.at[n], cy_r.at[n], core_id)

    def cy_in(n):
        return remote(part(c_yc, x, n), part(c_yc, x, n), cy_s.at[n], cy_r.at[n], core_id)

    def cx_copy(n):
        return remote(part(c_y, 1 - x, n), part(c_y, 1 - x, n), cx_s.at[n], cx_r.at[n], core_id)

    def cx_in(n):
        return remote(part(c_yc, 1 - x, n), part(c_yc, 1 - x, n), cx_s.at[n], cx_r.at[n], core_id)

    def pass_y(n):
        y_in(n).wait_recv()
        x_copy(n).start()
        cy_copy(n).start()

    def pass_x(n):
        x_in(n).wait_recv()
        cx_copy(n).start()

    def expand(block):
        rows = pl.ds(pl.multiple_of(block * tok, tok), tok)
        front = lat[block, :, :KVR]
        rope = lat[block, :, KVR:]
        for h in range(heads):
            cols = slice(h * (NOPE + VDIM), (h + 1) * (NOPE + VDIM))
            both = jnp.dot(front, ukv_ref[:, cols], preferred_element_type=F32).astype(BF16)
            keys[h, rows, :NOPE] = both[:, :NOPE]
            keys[h, rows, NOPE:] = rope
            values[h, rows, :] = both[:, NOPE:]

    expand(c)
    bias[...] = jnp.where(key_pos_ref[...] <= own_pos_ref[...], 0.0, -1e30).astype(F32)
    lat_copy(c_core, 0, core_id).wait_recv()
    expand(c_core)
    lat_copy(c_y, 1, y_id).wait_recv()
    lat_copy(c_y, 2, core_id).start()
    lat_copy(c, 1, y_id).wait_send()
    for n in range(chunks):
        y_copy(n).start()
    expand(c_y)
    lat_copy(c_yc, 2, core_id).wait_recv()
    expand(c_yc)

    scale = (NOPE + ROPE) ** (-0.5) * math.log2(math.e)
    for h in range(heads):
        q = q_ref[:, h * qd : (h + 1) * qd]
        q = jnp.concatenate([q, jnp.zeros((tok, 2 * NOPE - qd), BF16)], axis=1)
        scores = lax.dot_general(
            q, keys[h], (((1,), (1,)), ((), ())), preferred_element_type=F32
        )
        scores = scores * scale + bias[...]
        peak = jnp.max(scores, axis=1, keepdims=True)
        probs = jnp.exp2(scores - peak)
        total = jnp.sum(probs, axis=1, keepdims=True)
        summed = jnp.dot(probs.astype(BF16), values[h], preferred_element_type=F32)
        att[:, h * VDIM : (h + 1) * VDIM] = (summed / total).astype(BF16)

    pass_y(0)
    pass_y(1)
    pass_x(0)
    own_w.wait()
    own_to_core.wait_recv()

    def send(kind, n, slot, dev):
        return remote(
            outbox.at[kind, n], inbox.at[slot, n], ob_s.at[kind, n], ib_r.at[slot, n], (x, c, dev)
        )

    def arrived(slot, n):
        return remote(
            outbox.at[0, n], inbox.at[slot, n], ob_s.at[0, n], ib_r.at[slot, n], (x, c, partner)
        )

    def relay(n):
        for kind, dest in ((2, end_far), (1, mid_far)):
            arrived(1 + kind, n).wait_recv()
            outbox[kind, n] = (
                outbox[kind, n].astype(F32) + inbox[1 + kind, n].astype(F32)
            ).astype(BF16)
            send(kind, n, 1, dest).start()

    def step(n, carry):
        @pl.when(n + 2 < chunks)
        def _():
            pass_y(n + 2)

        @pl.when(n + 1 < chunks)
        def _():
            pass_x(n + 1)

        cy_in(n).wait_recv()
        cx_in(n).wait_recv()
        cols = pl.ds(pl.multiple_of(n * CW, CW), CW)

        def term(block):
            return jnp.dot(att[...], w[block, :, cols], preferred_element_type=F32)

        outbox[2, n] = term(end_far).astype(BF16)

        @pl.when(is_edge)
        def _():
            send(2, n, 3, partner).start()

        outbox[1, n] = term(mid_far).astype(BF16)

        @pl.when(is_edge)
        def _():
            send(1, n, 2, partner).start()

        outbox[0, n] = term(partner).astype(BF16)
        send(0, n, 0, partner).start()
        pown[n] = term(z)

        @pl.when(jnp.logical_and(jnp.logical_not(is_edge), n > 0))
        def _():
            relay(n - 1)

        return carry

    lax.fori_loop(0, chunks, step, 0)

    @pl.when(jnp.logical_not(is_edge))
    def _():
        relay(chunks - 1)

    for n in range(chunks):
        arrived(1, n).wait_recv()
        arrived(0, n).wait_recv()
        out_ref[:, n * CW : (n + 1) * CW] = (
            pown[n] + inbox[0, n].astype(F32) + inbox[1, n].astype(F32)
        ).astype(BF16)

    lat_copy(c, 0, core_id).wait_send()
    lat_copy(c_y, 2, core_id).wait_send()
    own_to_core.wait_send()

    def drain(n, carry):
        y_copy(n).wait_send()
        x_copy(n).wait_send()
        cy_copy(n).wait_send()
        cx_copy(n).wait_send()
        for kind in range(3):
            send(kind, n, 0, partner).wait_send()
        return carry

    lax.fori_loop(0, chunks, drain, 0)


def shards_fused(queries, kv_latent, kv_gain, w_ukv, w_out, row_position):
    tok = queries.shape[0]
    tokens = row_position.shape[0]
    heads = w_ukv.shape[1] // (NOPE + VDIM)
    depth, width = w_out.shape
    blocks = tokens // tok
    chunks = width // CW
    own_pos = lax.dynamic_slice_in_dim(row_position, lax.axis_index("ctx") * tok, tok)
    vmem = pl.BlockSpec(memory_space=pltpu.VMEM)
    dma = pltpu.SemaphoreType.DMA
    return pl.pallas_call(
        layer_kernel,
        out_shape=jax.ShapeDtypeStruct((tok, width), BF16),
        in_specs=[vmem] * 6 + [pl.BlockSpec(memory_space=pl.ANY)],
        out_specs=vmem,
        scratch_shapes=[
            pltpu.VMEM((blocks, tok, LAT), BF16),
            pltpu.VMEM((heads, tokens, 2 * NOPE), BF16),
            pltpu.VMEM((heads, tokens, VDIM), BF16),
            pltpu.VMEM((tok, tokens), F32),
            pltpu.VMEM((tok, heads * VDIM), BF16),
            pltpu.VMEM((blocks, depth, width), BF16),
            pltpu.VMEM((chunks, tok, CW), F32),
            pltpu.VMEM((3, chunks, tok, CW), BF16),
            pltpu.VMEM((4, chunks, tok, CW), BF16),
            dma,
            dma((3,)),
            dma((3,)),
            dma,
            dma,
        ]
        + [dma((chunks,))] * 8
        + [dma((3, chunks)), dma((4, chunks))],
        compiler_params=pltpu.CompilerParams(
            collective_id=0, has_side_effects=True, vmem_limit_bytes=56 * 1024 * 1024
        ),
        cost_estimate=pl.CostEstimate(
            flops=5_200_000_000, bytes_accessed=8_000_000, transcendentals=tok * tokens * heads
        ),
    )(
        queries, kv_latent, kv_gain.reshape(1, KVR), w_ukv, own_pos.reshape(tok, 1),
        row_position.reshape(1, tokens), w_out,
    )


def attend_piece(state, piece, key_pos, q_heads, own_pos, w_ukv):
    heads = q_heads.shape[1]
    length = piece.shape[0]
    factor_score = (NOPE + ROPE) ** (-0.5)
    for begin in range(0, length, 1024):
        size = min(1024, length - begin)
        rows = piece[begin : begin + size]
        positions = key_pos[begin : begin + size]
        peak, mass, acc = state
        expanded = jnp.dot(rows[:, :KVR], w_ukv, preferred_element_type=F32).astype(BF16)
        expanded = expanded.reshape(size, heads, NOPE + VDIM)
        scores = jnp.einsum(
            "qhd,khd->qhk", q_heads[:, :, :NOPE], expanded[:, :, :NOPE], preferred_element_type=F32
        )
        scores = scores + jnp.einsum(
            "qhd,kd->qhk", q_heads[:, :, NOPE:], rows[:, KVR:], preferred_element_type=F32
        )
        scores = scores * factor_score
        allowed = (positions[None, :] <= own_pos[:, None])[:, None, :]
        scores = jnp.where(allowed, scores, -1e30)
        new_peak = jnp.maximum(peak, jnp.max(scores, axis=2))
        shrink = jnp.exp(peak - new_peak)
        probs = jnp.where(allowed, jnp.exp(scores - new_peak[:, :, None]), 0.0)
        mass = mass * shrink + jnp.sum(probs, axis=2)
        added = jnp.einsum(
            "qhk,khd->qhd", probs.astype(BF16), expanded[:, :, NOPE:], preferred_element_type=F32
        )
        acc = acc * shrink[:, :, None] + added
        state = (new_peak, mass, acc)
    return state


def shards_general(queries, kv_latent, kv_gain, w_ukv, w_out, row_position):
    tok_rows = queries.shape[0]
    heads = w_ukv.shape[1] // (NOPE + VDIM)
    ctx_index = lax.axis_index("ctx")
    own_pos = lax.dynamic_slice_in_dim(row_position, ctx_index * tok_rows, tok_rows)
    latent = normalize(kv_latent, kv_gain)
    q_heads = queries.reshape(tok_rows, heads, NOPE + ROPE)
    start_state = (
        jnp.full((tok_rows, heads), -1e30, F32),
        jnp.zeros((tok_rows, heads), F32),
        jnp.zeros((tok_rows, heads, VDIM), F32),
    )
    every = lax.all_gather(latent, "ctx", axis=0, tiled=True)
    peak, mass, acc = attend_piece(start_state, every, row_position, q_heads, own_pos, w_ukv)
    attended = (acc / mass[:, :, None]).astype(BF16).reshape(tok_rows, heads * VDIM)
    terms = jnp.dot(
        attended, lax.all_gather(w_out, "ctx", axis=1, tiled=True), preferred_element_type=F32
    )
    return lax.psum_scatter(terms.astype(BF16), "head", scatter_dimension=1, tiled=True)


def solution(mesh):
    placed = (
        P(("seq", "ctx"), "head"),
        P(("seq", "ctx"), None),
        P(),
        P(None, "head"),
        P("head", "ctx"),
        P("seq"),
    )
    fused = (mesh.shape["seq"], mesh.shape["ctx"], mesh.shape["head"]) == (2, 4, 4)
    return jax.shard_map(
        shards_fused if fused else shards_general,
        mesh=mesh,
        in_specs=placed,
        out_specs=P(("seq", "ctx"), "head"),
        check_vma=False,
    )
```

time: 177 us -> 87.4 us (0.49)
  waiting for transfers between devices: 124 us -> 0 us
  Pallas kernels: 0 us -> 82.3 us
  matrix products: 16.3 us -> 0 us
  between operations: 13.6 us -> 0.01 us
  blocking collectives: 11.1 us -> 0 us
  local copies, waits for them, and re-layouts: 8.93 us -> 4.78 us
  other arithmetic: 2.04 us -> 0 us
    pallas_call x0 -> x1, Pallas kernels: none -> 82.3 us  [shards_fused(): pl.pallas_call(layer_kernel, out_shape=jax.ShapeDtypeStruct((tok, width),...]
    all_gather x1 -> x0, waiting for transfers between devices: 69.5 us -> none  [shards(): lax.all_gather(w_out, 'ctx', axis=1, tiled=True)]
    reduce_scatter x1 -> x0, waiting for transfers between devices: 54.3 us -> none  [shards(): lax.psum_scatter(terms.astype(jnp.bfloat16), 'head', scatter_dimension=1,...]
    dot_general x5 -> x0, matrix products: 16.3 us -> none  [the longest x1 9.69 us: shards(): jnp.dot(attended, lax.all_gather(w_out, 'ctx', axis=1, tiled=True), prefe...]
    all_gather x1 -> x0, blocking collectives: 11.1 us -> none  [shards(): every = lax.all_gather(latent, 'ctx', axis=0, tiled=True)]
    slice x7 -> x0, local copies, waits for them, and re-layouts: 2.93 us -> none  [the longest x1 2.73 us: attend_piece(): expanded[:, :, :NOPE]]
    unnamed x13 -> x1, local copies, waits for them, and re-layouts: 4.2 us -> 1.99 us
  transfers between devices with their start and end apart: 2 -> 0, of which waited for: 2 -> 0; matrix products, arithmetic and copies ran while one was open for 9% -> 0% of each run, Pallas kernels for 0% -> 0%
where the time goes in v1:
time: 87.4 us; the launch traced here: 87.1 us
  Pallas kernels  82.3 us (94%)
  local copies, waits for them, and re-layouts  4.78 us (5%)
    pallas_call x1, Pallas kernels, shards_fused(): pl.pallas_call(layer_kernel, out_shape=jax.ShapeDtypeStruct((tok, width),...  82.3 us
    unnamed x1, local copies, waits for them, and re-layouts  1.99 us

profile of v1, /device:TPU:0, one launch (start us, length us, event | category | flops | bytes accessed | tf_op | source)
XLA Modules:
  0.0 87.1 jit_solution(9612837317569840831)
XLA Ops:
  0.0 0.8 dynamic_slice.3
  0.8 1.3 %reshape.11.key_pos_ref = s32[1,768]{1,0:T(1,128)} reshape(s32[768]{0:T(1024)} %param.11) | data formatting | bytes 6144 | tf_op jit(solution)/shard_map/reshape | solution.py:297
  2.0 0.8 copy.7.own_pos_ref
  2.8 82.3 %shard_map.64 = bf16[192,1792]{1,0:T(8,128)(2,1)} custom-call(bf16[192,1536]{1,0:T(8,128)(2,1)} %q_ref.1, bf16[192,576]{1,0:T(8,128)(2,1)} %kvl_ref.1, f32[1,512]{1,0:T(1,128)} %bitcast.3, bf16[512,2048]{1,0:T(8,128)(2,1)} %ukv_ref.1, s32[192,1]{1,0:T(8,128)} %copy.7.own_pos_ref, s32[1,768]{1,0:T(1,128)} %reshape.11.key_pos_ref, bf16[1024,1792]{1,0:T(8,128)(2,1)} %wout_ref.1), custom_call_target="tpu_custom_call" | custom-call | flops 5200000000 | bytes 8000000 | tf_op jit(solution)/shard_map/pallas_call | solution.py:266
  85.1 2.0 %copy.9 = bf16[192,1792]{1,0:T(8,128)(2,1)} copy(bf16[192,1792]{1,0:T(8,128)(2,1)} %shard_map.64) | data formatting | bytes 1376256

commit v2 on v1

--- a/solution.py
+++ b/solution.py
@@ -26,9 +26,9 @@
 
 
 def layer_kernel(
-    q_ref, kvl_ref, gain_ref, ukv_ref, own_pos_ref, key_pos_ref, wout_ref, out_ref,
-    lat, keys, values, bias, att, w, pown, outbox, inbox,
-    local_sem, lat_s, lat_r, core_s, core_r, y_s, y_r, x_s, x_r, cy_s, cy_r, cx_s, cx_r, ob_s, ib_r,
+    kvl_ref, gain_ref, pos_ref, q_hbm, ukv_hbm, wout_ref, out_ref,
+    q_ref, ukv_ref, lat, keys, values, bias, att, w, pown, outbox, inbox,
+    local_sem, q_sem, ukv_sem, lat_s, lat_r, core_s, core_r, y_s, y_r, x_s, x_r, cy_s, cy_r, cx_s, cx_r, ob_s, ib_r,
 ):
     x = lax.axis_index("seq")
     c = lax.axis_index("ctx")
@@ -40,6 +40,7 @@
     c_yc = (1 - y) * 2 + (1 - k)
     side = z // 2
     is_edge = (z % 2) == side
+    near_first = side == y
     partner = z + 1 - 2 * (z % 2)
     mid_far = 2 - side
     end_far = 3 * (1 - side)
@@ -59,13 +60,17 @@
     for peer in (core_id, y_id, x_id, (x, c, partner), (x, c, mid_far), (x, c, end_far)):
         pl.semaphore_signal(barrier, inc=1, device_id=peer, device_id_type=pl.DeviceIdType.MESH)
 
+    load_ukv = pltpu.make_async_copy(ukv_hbm, ukv_ref, ukv_sem)
+    load_ukv.start()
+    load_q = pltpu.make_async_copy(q_hbm, q_ref, q_sem)
+    load_q.start()
     own_w = pltpu.make_async_copy(wout_ref, w.at[c], local_sem)
     own_w.start()
 
     raw = kvl_ref[...].astype(F32)
     front = raw[:, :KVR]
     factor = lax.rsqrt(jnp.mean(front * front, axis=1, keepdims=True) + 1e-06)
-    lat[c, :, :KVR] = (front * factor * gain_ref[...]).astype(BF16)
+    lat[c, :, :KVR] = (front * factor * gain_ref[...].reshape(1, KVR)).astype(BF16)
     lat[c, :, KVR:] = jnp.concatenate(
         [kvl_ref[:, KVR:], jnp.zeros((tok, LAT - KVR - ROPE), BF16)], axis=1
     )
@@ -83,7 +88,6 @@
     lat_copy(c, 1, y_id).start()
     lat_copy(c, 0, core_id).start()
     own_to_core = remote(wout_ref, w.at[c], core_s, core_r, core_id)
-    own_to_core.start()
 
     def part(block, which, n):
         rows = pl.ds(pl.multiple_of(which * half, half), half)
@@ -135,18 +139,26 @@
             keys[h, rows, NOPE:] = rope
             values[h, rows, :] = both[:, NOPE:]
 
+    for n in range(chunks):
+        y_copy(n).start()
+    own_to_core.start()
+
+    key_pos = pos_ref[...].astype(F32).reshape(1, pos_ref.shape[0])
+    shape = bias.shape
+    own_row = lax.broadcasted_iota(jnp.int32, shape, 0) + c * tok
+    is_own = lax.broadcasted_iota(jnp.int32, shape, 1) == own_row
+    own_pos = jnp.sum(jnp.where(is_own, key_pos, 0.0), axis=1, keepdims=True)
+    bias[...] = jnp.where(key_pos <= own_pos, 0.0, -1e30).astype(F32)
+    load_ukv.wait()
     expand(c)
-    bias[...] = jnp.where(key_pos_ref[...] <= own_pos_ref[...], 0.0, -1e30).astype(F32)
     lat_copy(c_core, 0, core_id).wait_recv()
     expand(c_core)
     lat_copy(c_y, 1, y_id).wait_recv()
     lat_copy(c_y, 2, core_id).start()
-    lat_copy(c, 1, y_id).wait_send()
-    for n in range(chunks):
-        y_copy(n).start()
     expand(c_y)
     lat_copy(c_yc, 2, core_id).wait_recv()
     expand(c_yc)
+    load_q.wait()
 
     scale = (NOPE + ROPE) ** (-0.5) * math.log2(math.e)
     for h in range(heads):
@@ -161,10 +173,9 @@
         total = jnp.sum(probs, axis=1, keepdims=True)
         summed = jnp.dot(probs.astype(BF16), values[h], preferred_element_type=F32)
         att[:, h * VDIM : (h + 1) * VDIM] = (summed / total).astype(BF16)
-
-    pass_y(0)
-    pass_y(1)
-    pass_x(0)
+        if h == heads // 2:
+            pass_y(0)
+
     own_w.wait()
     own_to_core.wait_recv()
 
@@ -186,7 +197,35 @@
             ).astype(BF16)
             send(kind, n, 1, dest).start()
 
-    def step(n, carry):
+    def term(block, n):
+        cols = pl.ds(pl.multiple_of(n * CW, CW), CW)
+        return jnp.dot(att[...], w[block, :, cols], preferred_element_type=F32)
+
+    def near(n):
+        outbox[0, n] = term(partner, n).astype(BF16)
+        send(0, n, 0, partner).start()
+        pown[n] = term(z, n)
+
+    def far(n):
+        for kind, dest in ((2, end_far), (1, mid_far)):
+            outbox[kind, n] = term(dest, n).astype(BF16)
+
+            @pl.when(is_edge)
+            def _():
+                send(kind, n, 1 + kind, partner).start()
+
+    def first(n, carry):
+        @pl.when(near_first)
+        def _():
+            near(n)
+
+        @pl.when(jnp.logical_not(near_first))
+        def _():
+            far(n)
+
+        return carry
+
+    def second(n, carry):
         @pl.when(n + 2 < chunks)
         def _():
             pass_y(n + 2)
@@ -197,37 +236,29 @@
 
         cy_in(n).wait_recv()
         cx_in(n).wait_recv()
-        cols = pl.ds(pl.multiple_of(n * CW, CW), CW)
-
-        def term(block):
-            return jnp.dot(att[...], w[block, :, cols], preferred_element_type=F32)
-
-        outbox[2, n] = term(end_far).astype(BF16)
-
-        @pl.when(is_edge)
-        def _():
-            send(2, n, 3, partner).start()
-
-        outbox[1, n] = term(mid_far).astype(BF16)
-
-        @pl.when(is_edge)
-        def _():
-            send(1, n, 2, partner).start()
-
-        outbox[0, n] = term(partner).astype(BF16)
-        send(0, n, 0, partner).start()
-        pown[n] = term(z)
-
-        @pl.when(jnp.logical_and(jnp.logical_not(is_edge), n > 0))
-        def _():
-            relay(n - 1)
+
+        @pl.when(near_first)
+        def _():
+            far(n)
+
+        @pl.when(jnp.logical_not(near_first))
+        def _():
+            near(n)
+
+        @pl.when(jnp.logical_and(jnp.logical_not(is_edge), n > 1))
+        def _():
+            relay(n - 2)
 
         return carry
 
-    lax.fori_loop(0, chunks, step, 0)
+    lax.fori_loop(0, chunks, first, 0)
+    pass_y(1)
+    pass_x(0)
+    lax.fori_loop(0, chunks, second, 0)
 
     @pl.when(jnp.logical_not(is_edge))
     def _():
+        relay(chunks - 2)
         relay(chunks - 1)
 
     for n in range(chunks):
@@ -238,6 +269,7 @@
         ).astype(BF16)
 
     lat_copy(c, 0, core_id).wait_send()
+    lat_copy(c, 1, y_id).wait_send()
     lat_copy(c_y, 2, core_id).wait_send()
     own_to_core.wait_send()
 
@@ -260,15 +292,16 @@
     depth, width = w_out.shape
     blocks = tokens // tok
     chunks = width // CW
-    own_pos = lax.dynamic_slice_in_dim(row_position, lax.axis_index("ctx") * tok, tok)
     vmem = pl.BlockSpec(memory_space=pltpu.VMEM)
     dma = pltpu.SemaphoreType.DMA
     return pl.pallas_call(
         layer_kernel,
         out_shape=jax.ShapeDtypeStruct((tok, width), BF16),
-        in_specs=[vmem] * 6 + [pl.BlockSpec(memory_space=pl.ANY)],
+        in_specs=[vmem] * 3 + [pl.BlockSpec(memory_space=pl.ANY)] * 3,
         out_specs=vmem,
         scratch_shapes=[
+            pltpu.VMEM(queries.shape, BF16),
+            pltpu.VMEM(w_ukv.shape, BF16),
             pltpu.VMEM((blocks, tok, LAT), BF16),
             pltpu.VMEM((heads, tokens, 2 * NOPE), BF16),
             pltpu.VMEM((heads, tokens, VDIM), BF16),
@@ -278,6 +311,8 @@
             pltpu.VMEM((chunks, tok, CW), F32),
             pltpu.VMEM((3, chunks, tok, CW), BF16),
             pltpu.VMEM((4, chunks, tok, CW), BF16),
+            dma,
+            dma,
             dma,
             dma((3,)),
             dma((3,)),
@@ -292,10 +327,7 @@
         cost_estimate=pl.CostEstimate(
             flops=5_200_000_000, bytes_accessed=8_000_000, transcendentals=tok * tokens * heads
         ),
-    )(
-        queries, kv_latent, kv_gain.reshape(1, KVR), w_ukv, own_pos.reshape(tok, 1),
-        row_position.reshape(1, tokens), w_out,
-    )
+    )(kv_latent, kv_gain, row_position, queries, w_ukv, w_out)
 
 
 def attend_piece(state, piece, key_pos, q_heads, own_pos, w_ukv):

time: 87.4 us -> 82.6 us (0.945)
  local copies, waits for them, and re-layouts: 4.78 us -> 1.99 us
  Pallas kernels: 82.3 us -> 80.5 us
    reshape x2 -> x0, local copies, waits for them, and re-layouts: 2.03 us -> none  [the longest x1 1.27 us: shards_fused(): row_position.reshape(1, tokens)]
    pallas_call x1, Pallas kernels: 82.3 us -> 80.5 us  [shards_fused(): pl.pallas_call(layer_kernel, out_shape=jax.ShapeDtypeStruct((tok, width),...]
where the time goes in v2:
time: 82.6 us; the launch traced here: 82.5 us
  Pallas kernels  80.5 us (97%)
  local copies, waits for them, and re-layouts  1.99 us (2%)
    pallas_call x1, Pallas kernels, shards_fused(): pl.pallas_call(layer_kernel, out_shape=jax.ShapeDtypeStruct((tok, width),...  80.5 us
    unnamed x1, local copies, waits for them, and re-layouts  1.99 us

profile of v2, /device:TPU:0, one launch (start us, length us, event | category | flops | bytes accessed | tf_op | source)
XLA Modules:
  0.0 82.5 jit_solution(18051317486632543693)
XLA Ops:
  0.0 80.5 %shard_map.64 = bf16[192,1792]{1,0:T(8,128)(2,1)} custom-call(bf16[192,576]{1,0:T(8,128)(2,1)} %kvl_ref.1, f32[512]{0:T(512)} %gain_ref.1, s32[768]{0:T(1024)} %pos_ref.1, bf16[192,1536]{1,0:T(8,128)(2,1)} %q_hbm.1, bf16[512,2048]{1,0:T(8,128)(2,1)} %ukv_hbm.1, bf16[1024,1792]{1,0:T(8,128)(2,1)} %wout_ref.1), custom_call_target="tpu_custom_call" | custom-call | flops 5200000000 | bytes 8000000 | tf_op jit(solution)/shard_map/pallas_call | solution.py:297
  80.5 2.0 %copy.8 = bf16[192,1792]{1,0:T(8,128)(2,1)} copy(bf16[192,1792]{1,0:T(8,128)(2,1)} %shard_map.64) | data formatting | bytes 1376256

commit v3 on v2

--- a/solution.py
+++ b/solution.py
@@ -13,7 +13,8 @@
 ROPE = 64
 VDIM = 128
 LAT = 640
-CW = 256
+CW = 128
+EARLY = 3
 F32 = jnp.float32
 BF16 = jnp.bfloat16
 
@@ -41,6 +42,7 @@
     side = z // 2
     is_edge = (z % 2) == side
     near_first = side == y
+    hold = jnp.logical_and(is_edge, near_first)
     partner = z + 1 - 2 * (z % 2)
     mid_far = 2 - side
     end_far = 3 * (1 - side)
@@ -65,7 +67,6 @@
     load_q = pltpu.make_async_copy(q_hbm, q_ref, q_sem)
     load_q.start()
     own_w = pltpu.make_async_copy(wout_ref, w.at[c], local_sem)
-    own_w.start()
 
     raw = kvl_ref[...].astype(F32)
     front = raw[:, :KVR]
@@ -142,6 +143,7 @@
     for n in range(chunks):
         y_copy(n).start()
     own_to_core.start()
+    own_w.start()
 
     key_pos = pos_ref[...].astype(F32).reshape(1, pos_ref.shape[0])
     shape = bias.shape
@@ -203,7 +205,11 @@
 
     def near(n):
         outbox[0, n] = term(partner, n).astype(BF16)
-        send(0, n, 0, partner).start()
+
+        @pl.when(jnp.logical_not(jnp.logical_and(hold, n >= EARLY)))
+        def _():
+            send(0, n, 0, partner).start()
+
         pown[n] = term(z, n)
 
     def far(n):
@@ -245,9 +251,13 @@
         def _():
             near(n)
 
-        @pl.when(jnp.logical_and(jnp.logical_not(is_edge), n > 1))
-        def _():
-            relay(n - 2)
+        @pl.when(jnp.logical_and(hold, n % 2 == 1))
+        def _():
+            send(0, EARLY + n // 2, 0, partner).start()
+
+        @pl.when(jnp.logical_and(jnp.logical_not(is_edge), n > 0))
+        def _():
+            relay(n - 1)
 
         return carry
 
@@ -258,8 +268,12 @@
 
     @pl.when(jnp.logical_not(is_edge))
     def _():
-        relay(chunks - 2)
         relay(chunks - 1)
+
+    @pl.when(hold)
+    def _():
+        for n in range(EARLY + chunks // 2, chunks):
+            send(0, n, 0, partner).start()
 
     for n in range(chunks):
         arrived(1, n).wait_recv()

time: 82.6 us -> 82 us (level)
  no operation moved by 1% of the time
where the time goes in v3:
time: 82 us; the launch traced here: 81.8 us
  Pallas kernels  79.8 us (97%)
  local copies, waits for them, and re-layouts  1.99 us (2%)
    pallas_call x1, Pallas kernels, shards_fused(): pl.pallas_call(layer_kernel, out_shape=jax.ShapeDtypeStruct((tok, width),...  79.8 us
    unnamed x1, local copies, waits for them, and re-layouts  1.99 us

profile of v3, /device:TPU:0, one launch (start us, length us, event | category | flops | bytes accessed | tf_op | source)
XLA Modules:
  0.0 81.8 jit_solution(14791974484860607573)
XLA Ops:
  0.0 79.8 %shard_map.64 = bf16[192,1792]{1,0:T(8,128)(2,1)} custom-call(bf16[192,576]{1,0:T(8,128)(2,1)} %kvl_ref.1, f32[512]{0:T(512)} %gain_ref.1, s32[768]{0:T(1024)} %pos_ref.1, bf16[192,1536]{1,0:T(8,128)(2,1)} %q_hbm.1, bf16[512,2048]{1,0:T(8,128)(2,1)} %ukv_hbm.1, bf16[1024,1792]{1,0:T(8,128)(2,1)} %wout_ref.1), custom_call_target="tpu_custom_call" | custom-call | flops 5200000000 | bytes 8000000 | tf_op jit(solution)/shard_map/pallas_call | solution.py:311
  79.8 2.0 %copy.8 = bf16[192,1792]{1,0:T(8,128)(2,1)} copy(bf16[192,1792]{1,0:T(8,128)(2,1)} %shard_map.64) | data formatting | bytes 1376256

commit v4 on v2

--- a/solution.py
+++ b/solution.py
@@ -65,7 +65,6 @@
     load_q = pltpu.make_async_copy(q_hbm, q_ref, q_sem)
     load_q.start()
     own_w = pltpu.make_async_copy(wout_ref, w.at[c], local_sem)
-    own_w.start()
 
     raw = kvl_ref[...].astype(F32)
     front = raw[:, :KVR]
@@ -142,6 +141,7 @@
     for n in range(chunks):
         y_copy(n).start()
     own_to_core.start()
+    own_w.start()
 
     key_pos = pos_ref[...].astype(F32).reshape(1, pos_ref.shape[0])
     shape = bias.shape
@@ -245,9 +245,9 @@
         def _():
             near(n)
 
-        @pl.when(jnp.logical_and(jnp.logical_not(is_edge), n > 1))
-        def _():
-            relay(n - 2)
+        @pl.when(jnp.logical_and(jnp.logical_not(is_edge), n > 0))
+        def _():
+            relay(n - 1)
 
         return carry
 
@@ -258,7 +258,6 @@
 
     @pl.when(jnp.logical_not(is_edge))
     def _():
-        relay(chunks - 2)
         relay(chunks - 1)
 
     for n in range(chunks):

time: 82.6 us -> 78.4 us (0.949)
  Pallas kernels: 80.5 us -> 76.2 us
    pallas_call x1, Pallas kernels: 80.5 us -> 76.2 us  [shards_fused(): pl.pallas_call(layer_kernel, out_shape=jax.ShapeDtypeStruct((tok, width),...]
where the time goes in v4:
time: 78.4 us; the launch traced here: 78.2 us
  Pallas kernels  76.2 us (97%)
  local copies, waits for them, and re-layouts  1.99 us (3%)
    pallas_call x1, Pallas kernels, shards_fused(): pl.pallas_call(layer_kernel, out_shape=jax.ShapeDtypeStruct((tok, width),...  76.2 us
    unnamed x1, local copies, waits for them, and re-layouts  1.99 us

profile of v4, /device:TPU:0, one launch (start us, length us, event | category | flops | bytes accessed | tf_op | source)
XLA Modules:
  0.0 78.2 jit_solution(1670633516327159668)
XLA Ops:
  0.0 76.2 %shard_map.64 = bf16[192,1792]{1,0:T(8,128)(2,1)} custom-call(bf16[192,576]{1,0:T(8,128)(2,1)} %kvl_ref.1, f32[512]{0:T(512)} %gain_ref.1, s32[768]{0:T(1024)} %pos_ref.1, bf16[192,1536]{1,0:T(8,128)(2,1)} %q_hbm.1, bf16[512,2048]{1,0:T(8,128)(2,1)} %ukv_hbm.1, bf16[1024,1792]{1,0:T(8,128)(2,1)} %wout_ref.1), custom_call_target="tpu_custom_call" | custom-call | flops 5200000000 | bytes 8000000 | tf_op jit(solution)/shard_map/pallas_call | solution.py:296
  76.3 2.0 %copy.8 = bf16[192,1792]{1,0:T(8,128)(2,1)} copy(bf16[192,1792]{1,0:T(8,128)(2,1)} %shard_map.64) | data formatting | bytes 1376256

commit v5 on v4

--- a/solution.py
+++ b/solution.py
@@ -225,7 +225,18 @@
 
         return carry
 
+    middle = jnp.logical_not(is_edge)
+    far_first = jnp.logical_not(near_first)
+
     def second(n, carry):
+        @pl.when(middle & far_first & (n > 0))
+        def _():
+            relay(n - 1)
+
+        @pl.when(middle & far_first & (n == chunks - 1))
+        def _():
+            relay(n)
+
         @pl.when(n + 2 < chunks)
         def _():
             pass_y(n + 2)
@@ -245,7 +256,7 @@
         def _():
             near(n)
 
-        @pl.when(jnp.logical_and(jnp.logical_not(is_edge), n > 0))
+        @pl.when(middle & near_first & (n > 0))
         def _():
             relay(n - 1)
 
@@ -256,7 +267,7 @@
     pass_x(0)
     lax.fori_loop(0, chunks, second, 0)
 
-    @pl.when(jnp.logical_not(is_edge))
+    @pl.when(middle & near_first)
     def _():
         relay(chunks - 1)
 

time: 78.4 us -> 77 us (0.982)
  the two profiles are of different devices: /device:TPU:0 before, /device:TPU:16 now
where the time goes in v5:
time: 77 us; the launch traced here: 76.8 us
  Pallas kernels  74.8 us (97%)
  local copies, waits for them, and re-layouts  1.99 us (3%)
    pallas_call x1, Pallas kernels, shards_fused(): pl.pallas_call(layer_kernel, out_shape=jax.ShapeDtypeStruct((tok, width),...  74.8 us
    unnamed x1, local copies, waits for them, and re-layouts  1.99 us

profile of v5, /device:TPU:16, one launch (start us, length us, event | category | flops | bytes accessed | tf_op | source)
XLA Modules:
  0.0 76.8 jit_solution(17134192900434290603)
XLA Ops:
  0.0 74.8 %shard_map.64 = bf16[192,1792]{1,0:T(8,128)(2,1)} custom-call(bf16[192,576]{1,0:T(8,128)(2,1)} %kvl_ref.1, f32[512]{0:T(512)} %gain_ref.1, s32[768]{0:T(1024)} %pos_ref.1, bf16[192,1536]{1,0:T(8,128)(2,1)} %q_hbm.1, bf16[512,2048]{1,0:T(8,128)(2,1)} %ukv_hbm.1, bf16[1024,1792]{1,0:T(8,128)(2,1)} %wout_ref.1), custom_call_target="tpu_custom_call" | custom-call | flops 5200000000 | bytes 8000000 | tf_op jit(solution)/shard_map/pallas_call | solution.py:307
  74.8 2.0 %copy.8 = bf16[192,1792]{1,0:T(8,128)(2,1)} copy(bf16[192,1792]{1,0:T(8,128)(2,1)} %shard_map.64) | data formatting | bytes 1376256
